TPU v7x, 128 devices: a whole 4x4x4 slice. The times are simulated.
128 devices in a mesh: sub: 8 (over y, core), beam: 16 (over x, z).
Axes of the slice: x: 4, y: 4, z: 4, core: 2. Of those that a mesh axis runs over, the one named last changes fastest.
Arguments:
- subimage: float32 [8, 256, 2, 16384], P('sub', 'beam'), may hold values from -6 to 6
- pulses: float32 [2, 8, 16, 16, 2, 16384], P(None, 'sub', 'beam'), may hold values from -6 to 6
- ingest_owner: int32 [2, 8], P(None, 'sub'), may hold values from 0 to 15
- weights: float32 [2, 8, 256, 2, 16], P(None, 'sub', 'beam'), may hold values from -1 to 1
- offsets: int32 [2, 8, 256], P(None, 'sub', 'beam'), may hold values from 0 to 256
- filter_taps: float32 [2, 8, 256, 8], P(None, 'sub', 'beam'), may hold values from -2 to 2
- cycles: int32 [2, 8, 256], P(None, 'sub', 'beam'), may hold values from 0 to 16383
- merge_phase: float32 [2, 8, 256], P(None, 'sub', 'beam'), may hold values from -3.140625 to 3.140625
- destination: int32 [256, 1], P('beam'), may hold values from 0 to 15; in each aligned block of 16 rows (0 to 15, 16 to 31, ...) at most 2 rows name the same one
Outputs:
- regrouped: float32 [8, 512, 2, 16384], P('sub', 'beam')
Inputs may be any that keep to these rules, and one draw needn't show every extreme that they name: `destination`: the same owners for every subaperture group; among the rows of one device at most 2 go to one owner, and exactly 2 to some owner.
All inputs are finite; a program needn't handle non-finite values.
Results may differ from a plain program's by a relative error of at most 0.0003.
Values sent between devices are 32-bit elements; how exact they have to be, the bound alone decides.
A program may use at most 128 MiB of HBM per device.

v0:
```python
import math

import jax
import jax.numpy as jnp
from jax import lax
from jax.sharding import PartitionSpec as P

CAP = 2
MAXOFF = 256


TWO_PI = 2.0 * math.pi


def broadcast(block, axis, holder):
    block = jnp.where(lax.axis_index(axis) == holder, block, jnp.zeros_like(block))
    return lax.psum(block, axis)


def partner_2(block, axis, bit):
    count = lax.axis_size(axis)
    route = []
    for low in range(count):
        high = low | 1 << bit
        if high != low and high < count:
            route += [(low, high), (high, low)]
    return lax.ppermute(block, axis, route)


def project_rows(received_block, coeffs):
    highest = lax.Precision.HIGHEST
    real_part = jnp.dot(coeffs[:, 0], received_block[:, 0], precision=highest) - jnp.dot(
        coeffs[:, 1], received_block[:, 1], precision=highest
    )
    imag_part = jnp.dot(coeffs[:, 0], received_block[:, 1], precision=highest) + jnp.dot(
        coeffs[:, 1], received_block[:, 0], precision=highest
    )
    return jnp.stack([real_part, imag_part], axis=1)


def interpolate(row_data, shifts, filters):
    length = row_data.shape[2]
    tap_count = filters.shape[1]
    margin = MAXOFF + tap_count - 1
    shifted = jnp.pad(row_data, ((0, 0), (0, 0), (0, margin)))
    for bit_index in range(MAXOFF.bit_length()):
        step_size = 2**bit_index
        moved = jnp.concatenate(
            [shifted[:, :, step_size:], jnp.zeros((shifted.shape[0], 2, step_size), jnp.float32)],
            axis=2,
        )
        taken = shifts >> bit_index & 1 == 1
        shifted = jnp.where(taken[:, None, None], moved, shifted)
    summed = filters[:, 0, None, None] * shifted[:, :, 0:length]
    for tap_index in range(1, tap_count):
        summed = (
            summed
            + filters[:, tap_index, None, None] * shifted[:, :, tap_index : tap_index + length]
        )
    return summed


def apply_ramp(row_data, counts):
    length = row_data.shape[2]
    positions = jnp.arange(length, dtype=jnp.int32)
    ramp_angle = (counts[:, None] * positions[None, :] % length).astype(jnp.float32) * (
        TWO_PI / length
    )
    cos_part = jnp.cos(ramp_angle)
    sin_part = jnp.sin(ramp_angle)
    real_part = row_data[:, 0] * cos_part - row_data[:, 1] * sin_part
    imag_part = row_data[:, 0] * sin_part + row_data[:, 1] * cos_part
    return jnp.stack([real_part, imag_part], axis=1)


def rotate_add(own_rows, partner, phase_angle):
    cos_part = jnp.cos(phase_angle)[:, None]
    sin_part = jnp.sin(phase_angle)[:, None]
    real_part = partner[:, 0] * cos_part - partner[:, 1] * sin_part
    imag_part = partner[:, 0] * sin_part + partner[:, 1] * cos_part
    return own_rows + jnp.stack([real_part, imag_part], axis=1)


def place_by_table(table, rows):
    return jnp.einsum("sg,gcr->scr", table, rows, precision=lax.Precision.HIGHEST)


def add_block(current, pulses, ingest_owner, weights, offsets, filter_taps, cycles, section_index):
    received_block = broadcast(pulses[section_index, 0, 0], "beam", ingest_owner[section_index, 0])
    projected = project_rows(received_block, weights[section_index, 0])
    banded = interpolate(projected, offsets[section_index, 0], filter_taps[section_index, 0])
    return current + apply_ramp(banded, cycles[section_index, 0])


def per_device(
    subimage, pulses, ingest_owner, weights, offsets, filter_taps, cycles, merge_phase, destination
):
    beam_count = lax.axis_size("beam")
    row_count = subimage.shape[1]
    length = subimage.shape[3]
    current = add_block(subimage[0], pulses, ingest_owner, weights, offsets, filter_taps, cycles, 0)
    partner = partner_2(current, "sub", 0)
    current = rotate_add(current, partner, merge_phase[0, 0])
    current = add_block(current, pulses, ingest_owner, weights, offsets, filter_taps, cycles, 1)
    targets = destination[:, 0]
    same_owner = targets[:, None] == targets[None, :]
    earlier = (
        jnp.arange(row_count, dtype=jnp.int32)[None, :]
        < jnp.arange(row_count, dtype=jnp.int32)[:, None]
    )
    earlier_count = jnp.sum((same_owner & earlier).astype(jnp.int32), axis=1)
    slot_index = targets * CAP + earlier_count
    slot_numbers = jnp.arange(beam_count * CAP, dtype=jnp.int32)
    slot_table = (slot_numbers[:, None] == slot_index[None, :]).astype(jnp.float32)
    partner = partner_2(current, "sub", 1)
    merged = rotate_add(current, partner, merge_phase[1, 0])
    buffer = place_by_table(slot_table, merged).reshape(beam_count, CAP, 2, length)
    routed = lax.all_to_all(buffer, "beam", split_axis=0, concat_axis=0, tiled=True)
    result = routed.reshape(beam_count * CAP, 2, length)
    return result[None]


def solution(mesh):
    in_specs = (
        P("sub", "beam", None, None),
        P(None, "sub", "beam", None, None, None),
        P(None, "sub"),
        P(None, "sub", "beam", None, None),
        P(None, "sub", "beam"),
        P(None, "sub", "beam", None),
        P(None, "sub", "beam"),
        P(None, "sub", "beam"),
        P("beam", None),
    )
    out_specs = P("sub", "beam", None, None)
    return jax.shard_map(
        per_device, mesh=mesh, in_specs=in_specs, out_specs=out_specs, check_vma=False
    )
```

profile of v0, /device:TPU:0, one launch (start us, length us, event | category | flops | bytes accessed | tf_op | source)
XLA Modules:
  0.0 297.4 jit_solution(3046612963431418227)
XLA Ops:
  6.5 1.3 fusion.83
  9.1 5.4 %select_bitcast_fusion = (f32[16,2,16384]{2,1,0:T(2,128)}, f32[16,2,16384]{2,1,0:T(2,128)}) fusion(f32[2,1,1,16,2,16384]{5,4,3,2,1,0:T(2,128)} %param.10, pred[]{:T(512)S(6)} %eq.272, pred[]{:T(512)S(6)} %eq.253), kind=kLoop, calls=%fused_computation.79 | loop fusion | flops 1048576 | bytes 8388610 | tf_op jit(solution)/shard_map/jit(_where)/select_n | solution.py:16
  14.5 0.6 copy-done.7
  15.3 105.6 %all-reduce.23.cloned.1.call-done = (f32[16,2,16384]{2,1,0:T(2,128)}, f32[16,2,16384]{2,1,0:T(2,128)}) async-done(((f32[16,2,16384]{2,1,0:T(2,128)}, f32[16,2,16384]{2,1,0:T(2,128)}), (f32[16,2,16384]{2,1,0:T(2,128)}, f32[16,2,16384]{2,1,0:T(2,128)})) %all-reduce.23.cloned.1.call-update) | async-done | bytes 4194320 | tf_op jit(solution)/shard_map/psum | solution.py:17
  120.9 8.6 %fusion.79 = (f32[16,1,16384]{2,1,0:T(1,128)S(1)}, f32[16,1,16384]{2,1,0:T(1,128)S(1)}, f32[16,1,16384]{2,1,0:T(1,128)S(1)}, f32[16,1,16384]{2,1,0:T(1,128)S(1)}) fusion(f32[16,2,16384]{2,1,0:T(2,128)} %get-tuple-element.6, f32[16,2,16384]{2,1,0:T(2,128)} %get-tuple-element.5), kind=kLoop, calls=%fused_computation.186 | loop fusion | bytes 8388608 | tf_op jit(solution)/shard_map/slice | solution.py:32
  129.6 1.6 fusion.43
  131.2 1.6 fusion.47
  132.8 1.6 fusion
  134.4 1.6 fusion.1
  136.0 0.1 select_maximum_fusion
  136.2 0.6 slice.365
  136.8 0.3 pad_select_fusion.8
  137.1 0.6 slice.366
  137.7 0.4 pad_select_fusion.7
  138.1 0.6 slice.367
  138.7 0.3 pad_select_fusion.6
  139.0 0.6 slice.368
  139.6 0.3 pad_select_fusion.5
  139.9 0.6 slice.369
  140.5 0.3 pad_select_fusion.4
  140.7 0.6 slice.370
  141.4 0.3 pad_select_fusion.3
  141.6 0.8 slice.371
  142.4 0.3 pad_select_fusion.2
  142.8 0.3 pad_select_fusion.1
  143.1 1.6 fusion.53
  144.8 1.6 fusion.49
  146.4 1.6 fusion.3
  148.0 1.6 fusion.2
  149.6 0.1 select_maximum_fusion.1
  149.8 0.6 slice.340
  150.4 0.3 pad_select_fusion.17
  150.6 0.6 slice.341
  151.3 0.4 pad_select_fusion.16
  151.6 0.6 slice.342
  152.2 0.3 pad_select_fusion.15
  152.6 0.6 slice.343
  153.2 0.3 pad_select_fusion.14
  153.5 0.6 slice.344
  154.1 0.3 pad_select_fusion.13
  154.4 0.6 slice.345
  155.0 0.5 pad_select_fusion.12
  155.5 0.6 slice.346
  156.1 0.3 pad_select_fusion.11
  156.5 0.3 pad_select_fusion.10
  156.9 0.3 pad_select_fusion.9
  157.2 4.0 %fusion.11 = f32[16,2,16384]{2,0,1:T(8,128)S(1)} fusion(f32[16,2,16647]{2,0,1:T(8,128)S(1)} %pad_select_fusion.9, f32[16]{0:T(128)S(1)} %get-tuple-element.81, f32[16]{0:T(128)S(1)} %get-tuple-element.80, f32[16]{0:T(128)S(1)} %get-tuple-element.79, f32[16]{0:T(128)S(1)} %get-tuple-element.78, f32[16]{0:T(128)S(1)} %get-tuple-element.77, ...), kind=kLoop, calls=%fused_computation.45 | loop fusion | flops 7864320 | bytes 18874880 | tf_op jit(solution)/shard_map/add | solution.py:57
  161.2 4.7 %multiply_subtract_fusion.2 = (f32[16,1,16384]{2,0,1:T(8,128)S(1)}, f32[16,1,16384]{2,0,1:T(8,128)S(1)}) fusion(f32[16,2,16384]{2,0,1:T(8,128)S(1)} %fusion.11, s32[16]{0:T(128)S(1)} %get-tuple-element.50), kind=kLoop, calls=%fused_computation.115 | loop fusion | flops 5242880 | bytes 4194368 | tf_op jit(solution)/shard_map/sub | solution.py:71
  165.9 1.3 maximum_add_fusion.1
  167.3 0.2 copy-done.1
  167.5 0.6 slice-done
  168.1 0.3 pad_select_fusion
  168.4 4.0 %fusion.4 = f32[16,2,16384]{2,0,1:T(8,128)S(1)} fusion(f32[16,2,16647]{2,0,1:T(8,128)S(1)} %pad_select_fusion, f32[16]{0:T(128)S(1)} %get-tuple-element.30, f32[16]{0:T(128)S(1)} %get-tuple-element.31, f32[16]{0:T(128)S(1)} %get-tuple-element.32, f32[16]{0:T(128)S(1)} %get-tuple-element.33, f32[16]{0:T(128)S(1)} %get-tuple-element.34, ...), kind=kLoop, calls=%fused_computation.30 | loop fusion | flops 7864320 | bytes 18874880 | tf_op jit(solution)/shard_map/add | solution.py:57
  172.4 4.7 %multiply_subtract_fusion = (f32[16,1,16384]{2,0,1:T(8,128)S(1)}, f32[16,1,16384]{2,0,1:T(8,128)S(1)}) fusion(f32[16,2,16384]{2,0,1:T(8,128)S(1)} %fusion.4, s32[16]{0:T(128)S(1)} %get-tuple-element.49), kind=kLoop, calls=%fused_computation.109 | loop fusion | flops 5242880 | bytes 4194368 | tf_op jit(solution)/shard_map/sub | solution.py:71
  177.1 0.3 multiply_subtract_fusion.1
  177.4 1.4 fusion.32
  178.9 1.8 collective-permute-start.1
  180.7 0.2 convert_reduce_fusion
  180.9 45.5 %collective-permute-done.1 = f32[16,2,16384]{2,0,1:T(8,128)S(1)} collective-permute-done((f32[16,2,16384]{2,0,1:T(8,128)S(1)}, f32[16,2,16384]{2,0,1:T(8,128)S(1)}, u32[]{:S(2)}, u32[]{:S(2)}) %collective-permute-start.1) | collective-permute-done | bytes 2097184 | tf_op jit(solution)/shard_map/ppermute | solution.py:27
  226.4 0.3 subtract_bitcast_fusion
  226.7 3.1 %fusion.22 = f32[16,2,2,16384]{3,0,2,1:T(8,128)S(1)} fusion(f32[1,16,1,16384]{3,1,2,0:T(8,128)S(1)} %bitcast.169, f32[1,16,1,16384]{3,1,2,0:T(8,128)S(1)} %bitcast.168, f32[1,16,1,16384]{3,1,2,0:T(8,128)S(1)} %bitcast.174, f32[1,16,1,16384]{3,1,2,0:T(8,128)S(1)} %bitcast.173, f32[1,16,1,16384]{3,1,2,0:T(8,128)S(1)} %bitcast.172, ...), kind=kOutput, calls=%fused_computation.64 | convolution fusion | flops 205521408 | bytes 14680256 | tf_op jit(solution)/shard_map/sg,gcr->scr/dot_general | solution.py:85
  229.8 3.2 %copy.20 = f32[16,2,2,16384]{3,2,1,0:T(2,128)S(1)} copy(f32[16,2,2,16384]{3,0,2,1:T(8,128)S(1)} %fusion.22) | data formatting | bytes 8388608 | tf_op jit(solution)/shard_map/sg,gcr->scr/dot_general | solution.py:85
  233.1 55.2 %all_to_all.5 = f32[16,2,2,16384]{3,2,1,0:T(2,128)S(1)} all-to-all(f32[16,2,2,16384]{3,2,1,0:T(2,128)S(1)} %copy.20), channel_id=1, replica_groups=mesh['sub'=8,'beam'=16] {'beam'}, dimensions={0} | all-to-all | bytes 8388608 | tf_op jit(solution)/shard_map/all_to_all | solution.py:118
  288.3 2.0 copy.68
  (33 shorter events, 0.7 us)
Async XLA Ops:
  6.5 114.4 %all-reduce.23.cloned.1.call-start = ((), (), s32[]{:S(2)}) async-start(), calls=%async_computation.1 | async-start | bytes 8388608 | tf_op jit(solution)/shard_map/psum | solution.py:17
  14.4 0.7 copy-start.7
  14.4 0.7 copy-start.5
  14.5 0.7 copy-start.6
  14.5 0.8 copy-start.4
  14.5 0.8 copy-start.3
  143.1 1.6 copy-start
  161.2 4.7 %copy-start.2 = (f32[1,16,2,16384]{3,2,1,0:T(2,128)S(1)}, f32[1,16,2,16384]{3,2,1,0:T(2,128)}, u32[]{:S(2)}) copy-start(f32[1,16,2,16384]{3,2,1,0:T(2,128)} %param.9) | copy-start | bytes 6291460
  165.9 1.6 copy-start.1
  165.9 2.2 slice-start
  167.2 9.9 %collective-permute-start = (f32[16,2,16384]{2,0,1:T(8,128)S(1)}, f32[16,2,16384]{2,0,1:T(8,128)S(1)}, u32[]{:S(2)}, u32[]{:S(2)}) collective-permute-start(f32[16,2,16384]{2,0,1:T(8,128)S(1)} %maximum_add_fusion.1), channel_id=1, source_target_pairs={{0,16},{16,0},{32,48},{48,32},{64,80},{80,64},{96,112},{112,96},{1... | collective-permute-start | bytes 6291464 | tf_op jit(solution)/shard_map/ppermute | solution.py:27
  177.4 3.3 %copy-start.8 = (s32[16,1]{0,1:T(1,128)S(1)}, s32[16,1]{0,1:T(1,128)}, u32[]{:S(2)}) copy-start(s32[16,1]{0,1:T(1,128)} %param.17) | copy-start | bytes 196
  178.9 47.5 %collective-permute-start.1 = (f32[16,2,16384]{2,0,1:T(8,128)S(1)}, f32[16,2,16384]{2,0,1:T(8,128)S(1)}, u32[]{:S(2)}, u32[]{:S(2)}) collective-permute-start(f32[16,2,16384]{2,0,1:T(8,128)S(1)} %fusion.32), channel_id=1, source_target_pairs={{0,32},{32,0},{16,48},{48,16},{64,96},{96,64},{80,112},{112,80},{1... | collective-permute-start | bytes 6291464 | tf_op jit(solution)/shard_map/ppermute | solution.py:27
Sparse Core Ops, SparseCore 0:
  14.6 106.2 all-reduce.22
where the time goes:
time: 301 us; the launch traced here: 297 us
  waiting for transfers between devices  151 us (50%)
  blocking collectives  55.2 us (18%)
  other arithmetic  31.8 us (11%)
  local copies, waits for them, and re-layouts  26 us (9%)
  matrix products  16 us (5%)
  between operations  15.4 us (5%)
    psum x1, waiting for transfers between devices, broadcast(): return lax.psum(block, axis)  106 us
    all_to_all x1, blocking collectives, per_device(): lax.all_to_all(buffer, 'beam', split_axis=0, concat_axis=0, tiled=True)  55.2 us
    ppermute x2, waiting for transfers between devices, partner_2(): return lax.ppermute(block, axis, route)  45.5 us
    slice x19, local copies, waits for them, and re-layouts, interpolate(): shifted[:, :, step_size:]  9.84 us
    sub x2, other arithmetic, apply_ramp(): real_part = row_data[:, 0] * cos_part - row_data[:, 1] * sin_part  9.38 us
    slice x1, local copies, waits for them, and re-layouts, project_rows(): received_block[:, 0]  8.63 us
    add x2, other arithmetic, interpolate(): summed + filters[:, tap_index, None, None] * shifted[:, :, tap_index:tap_...  7.94 us
  transfers between devices with their start and end apart: 3, of which 2 were waited for; matrix products, arithmetic and copies ran while one was open for 3% of the time, Pallas kernels for 0%

commit v1 on v0

v1 whole, which is shorter than its diff:
```python
import functools
import math

import jax
import jax.numpy as jnp
from jax import lax
from jax.experimental import pallas as pl
from jax.experimental.pallas import tpu as pltpu
from jax.sharding import PartitionSpec as P

CAP = 2
TAPS = 8
PB = 16
ROWS = 16
BEAMS = 16
LANES = 128
SUBL = 256
PAD = 32
CHUNKS = 8
CS = SUBL // CHUNKS
TWO_PI = 2.0 * math.pi
MESH = pl.DeviceIdType.MESH


def swapped(x):
    n = x.shape[0] // 8
    y = x.reshape(n, 8, LANES)
    even = lax.broadcasted_iota(jnp.int32, (n, 8, LANES), 1) % 2 == 0
    z = jnp.where(even, pltpu.roll(y, 7, 1), pltpu.roll(y, 1, 1))
    return z.reshape(x.shape)


def pair_sign(rows):
    even = lax.broadcasted_iota(jnp.int32, (rows, LANES), 0) % 2 == 0
    return jnp.where(even, -1.0, 1.0).astype(jnp.float32)


def merge_kernel(
    weights, offsets, taps, block_cos, block_sin, turn_cos, turn_sin, slot_row, slot_used,
    sub_ref, got_ref, cos_ref, sin_ref,
    out_ref,
    proj, first, first_in, late, second, second_in, merged, slots,
    core_send, core_recv, y_send, y_recv, beam_send, beam_recv, own_sem,
):
    sub = lax.axis_index("sub")
    me = lax.axis_index("beam")
    core_peer = (sub ^ 1, me)
    y_peer = (sub ^ 2, me)

    barrier = pltpu.get_barrier_semaphore()
    pl.semaphore_signal(barrier, inc=1, device_id=core_peer, device_id_type=MESH)
    pl.semaphore_signal(barrier, inc=1, device_id=y_peer, device_id_type=MESH)
    for shift in range(1, BEAMS):
        pl.semaphore_signal(barrier, inc=1, device_id=(sub, me ^ shift), device_id_type=MESH)

    zero = jnp.zeros((PAD, LANES), jnp.float32)
    for s in range(2):
        def clear(g, _, s=s):
            proj[s, g, pl.ds(SUBL, PAD), :] = zero
            return 0
        lax.fori_loop(0, ROWS, clear, 0)

    def project(s, lo):
        def half(h, _):
            acc = [None] * 8
            for p in range(PB):
                b = got_ref[s, p, pl.ds(lo, CS), :]
                t = swapped(b) * pair_sign(CS)
                for k in range(8):
                    at = ((s * ROWS) + h * 8 + k) * 32 + p
                    term = weights[at] * b + weights[at + 16] * t
                    acc[k] = term if acc[k] is None else acc[k] + term
            for k in range(8):
                proj[s, h * 8 + k, pl.ds(lo, CS), :] = acc[k]
            return 0
        lax.fori_loop(0, 2, half, 0)

    lane = lax.broadcasted_iota(jnp.int32, (CS, LANES), 1)
    lane_w = lax.broadcasted_iota(jnp.int32, (CS + 8, LANES), 1)

    def added(s, g, lo):
        off = offsets[s * ROWS + g]
        a = off // LANES
        b = off % LANES
        v = proj[s, g, pl.ds(lo + 2 * a, CS + 8), :]
        u = pltpu.roll(v, lax.rem(LANES - b, LANES), 1)
        up = jnp.concatenate([u[2:], u[:2]], axis=0)
        w = jnp.where(lane_w < LANES - b, u, up)
        here, following = w[:CS], w[2 : CS + 2]
        base = (s * ROWS + g) * TAPS
        acc = taps[base] * here
        for k in range(1, TAPS):
            acc = acc + taps[base + k] * pltpu.roll(jnp.where(lane < k, following, here), LANES - k, 1)
        c0 = cos_ref[s, g]
        s0 = sin_ref[s, g]
        sign = pair_sign(8)
        parts = []
        turned = swapped(acc)
        for v8 in range(CS // 8):
            at = (s * ROWS + g) * (SUBL // 8) + lo // 8 + v8
            ci = block_cos[at]
            si = block_sin[at]
            cc = c0 * ci - s0 * si
            ss = (s0 * ci + c0 * si) * sign
            parts.append(acc[v8 * 8 : v8 * 8 + 8] * cc + turned[v8 * 8 : v8 * 8 + 8] * ss)
        return jnp.concatenate(parts, axis=0)

    def copy_core(c):
        return pltpu.make_async_remote_copy(
            src_ref=first.at[:, pl.ds(c * CS, CS), :], dst_ref=first_in.at[:, pl.ds(c * CS, CS), :],
            send_sem=core_send.at[c], recv_sem=core_recv.at[c], device_id=core_peer, device_id_type=MESH)

    def copy_y(c):
        return pltpu.make_async_remote_copy(
            src_ref=second.at[:, pl.ds(c * CS, CS), :], dst_ref=second_in.at[:, pl.ds(c * CS, CS), :],
            send_sem=y_send.at[c], recv_sem=y_recv.at[c], device_id=y_peer, device_id_type=MESH)

    def copy_own(c):
        return pltpu.make_async_copy(
            slots.at[pl.ds(me * CAP, CAP), pl.ds(c * CS, CS), :],
            out_ref.at[pl.ds(me * CAP, CAP), pl.ds(c * CS, CS), :], own_sem.at[c])

    sign = pair_sign(CS)

    def finish(c):
        lo = c * CS
        copy_y(c).wait_recv()

        def row(g, _):
            got = second_in[g, pl.ds(lo, CS), :]
            at = ROWS + g
            merged[g] = second[g, pl.ds(lo, CS), :] + got * turn_cos[at] + swapped(got) * (turn_sin[at] * sign)
            return 0
        lax.fori_loop(0, ROWS, row, 0)

        def slot(q, _):
            value = merged[slot_row[q]]
            slots[q, pl.ds(lo, CS), :] = jnp.where(slot_used[q] > 0, value, 0.0)
            return 0
        lax.fori_loop(0, BEAMS * CAP, slot, 0)

        def send(shift, _):
            to = me ^ shift
            pltpu.make_async_remote_copy(
                src_ref=slots.at[pl.ds(to * CAP, CAP), pl.ds(lo, CS), :],
                dst_ref=out_ref.at[pl.ds(me * CAP, CAP), pl.ds(lo, CS), :],
                send_sem=beam_send, recv_sem=beam_recv, device_id=(sub, to), device_id_type=MESH).start()
            return 0
        lax.fori_loop(1, BEAMS, send, 0)
        copy_own(c).start()

    project(0, 0)
    project(1, 0)
    for c in range(CHUNKS):
        lo = c * CS
        if c + 1 < CHUNKS:
            project(0, lo + CS)

        def row0(g, _, lo=lo):
            first[g, pl.ds(lo, CS), :] = sub_ref[g, pl.ds(lo, CS), :] + added(0, g, lo)
            return 0
        lax.fori_loop(0, ROWS, row0, 0)
        if c == 0:
            pl.semaphore_wait(barrier, BEAMS + 1)
        copy_core(c).start()
        if c + 1 < CHUNKS:
            project(1, lo + CS)

        def row1(g, _, lo=lo):
            late[g] = added(1, g, lo)
            return 0
        lax.fori_loop(0, ROWS, row1, 0)
        copy_core(c).wait_recv()

        def turn0(g, _, lo=lo):
            got = first_in[g, pl.ds(lo, CS), :]
            second[g, pl.ds(lo, CS), :] = (
                first[g, pl.ds(lo, CS), :] + late[g]
                + got * turn_cos[g] + swapped(got) * (turn_sin[g] * sign))
            return 0
        lax.fori_loop(0, ROWS, turn0, 0)
        copy_y(c).start()
        if c >= 1:
            finish(c - 1)
    finish(CHUNKS - 1)
    for c in range(CHUNKS):
        copy_core(c).wait_send()
        copy_y(c).wait_send()
        copy_own(c).wait()
    rest = slots.at[pl.ds(0, (BEAMS - 1) * CAP)]
    pltpu.make_async_copy(rest, rest, beam_send).wait()
    landed = out_ref.at[pl.ds(0, (BEAMS - 1) * CAP)]
    pltpu.make_async_copy(landed, landed, beam_recv).wait()


def merge_call(scalars, rows, got, cos_table, sin_table):
    smem = pl.BlockSpec(memory_space=pltpu.SMEM)
    vmem = pl.BlockSpec(memory_space=pltpu.VMEM)
    full = (ROWS, SUBL, LANES)
    return pl.pallas_call(
        merge_kernel,
        out_shape=jax.ShapeDtypeStruct((BEAMS * CAP, SUBL, LANES), jnp.float32),
        in_specs=[smem] * 9 + [vmem] * 4,
        out_specs=pl.BlockSpec(memory_space=pl.ANY),
        scratch_shapes=[
            pltpu.VMEM((2, ROWS, SUBL + PAD, LANES), jnp.float32),
            pltpu.VMEM(full, jnp.float32),
            pltpu.VMEM(full, jnp.float32),
            pltpu.VMEM((ROWS, CS, LANES), jnp.float32),
            pltpu.VMEM(full, jnp.float32),
            pltpu.VMEM(full, jnp.float32),
            pltpu.VMEM((ROWS, CS, LANES), jnp.float32),
            pltpu.VMEM((BEAMS * CAP, SUBL, LANES), jnp.float32),
            pltpu.SemaphoreType.DMA((CHUNKS,)),
            pltpu.SemaphoreType.DMA((CHUNKS,)),
            pltpu.SemaphoreType.DMA((CHUNKS,)),
            pltpu.SemaphoreType.DMA((CHUNKS,)),
            pltpu.SemaphoreType.DMA,
            pltpu.SemaphoreType.DMA,
            pltpu.SemaphoreType.DMA((CHUNKS,)),
        ],
        compiler_params=pltpu.CompilerParams(
            collective_id=1, has_side_effects=True, vmem_limit_bytes=48 * 2**20
        ),
    )(*scalars, rows, got, cos_table, sin_table)


def paired(x):
    lead = x.shape[:-2]
    n = len(lead)
    y = x.reshape(*lead, 2, SUBL // 2, LANES)
    y = y.transpose(*range(n), n + 1, n, n + 2)
    return y.reshape(*lead, SUBL, LANES)


def ramp_tables(cycles):
    length = SUBL // 2 * LANES
    scale = TWO_PI / length
    blocks = jnp.arange(SUBL // 8, dtype=jnp.int32) * (4 * LANES)
    coarse = (cycles[:, :, None] * blocks % length).astype(jnp.float32) * scale
    place = (
        jnp.arange(8, dtype=jnp.int32)[:, None] // 2 * LANES
        + jnp.arange(LANES, dtype=jnp.int32)[None, :]
    )
    fine = (cycles[:, :, None, None] * place % length).astype(jnp.float32) * scale
    return jnp.cos(coarse), jnp.sin(coarse), jnp.cos(fine), jnp.sin(fine)


def per_device(
    subimage, pulses, ingest_owner, weights, offsets, filter_taps, cycles, merge_phase, destination
):
    me = lax.axis_index("beam")
    mine = (ingest_owner[:, 0] == me)[:, None, None, None]
    block = paired(pulses[:, 0, 0])
    got = lax.psum(jnp.where(mine, block, 0.0), "beam")
    coarse_cos, coarse_sin, fine_cos, fine_sin = ramp_tables(cycles[:, 0])
    targets = destination[:, 0]
    same_owner = targets[:, None] == targets[None, :]
    order = jnp.arange(ROWS, dtype=jnp.int32)
    rank = jnp.sum((same_owner & (order[None, :] < order[:, None])).astype(jnp.int32), axis=1)
    table = jnp.arange(BEAMS * CAP, dtype=jnp.int32)[:, None] == (targets * CAP + rank)[None, :]
    slot_row = jnp.sum(jnp.where(table, order[None, :], 0), axis=1)
    slot_used = jnp.sum(table.astype(jnp.int32), axis=1)
    scalars = (
        weights[:, 0].reshape(-1),
        offsets[:, 0].reshape(-1),
        filter_taps[:, 0].reshape(-1),
        coarse_cos.reshape(-1),
        coarse_sin.reshape(-1),
        jnp.cos(merge_phase[:, 0]).reshape(-1),
        jnp.sin(merge_phase[:, 0]).reshape(-1),
        slot_row,
        slot_used,
    )
    out = merge_call(scalars, paired(subimage[0]), got, fine_cos, fine_sin)
    out = out.reshape(BEAMS * CAP, SUBL // 2, 2, LANES).transpose(0, 2, 1, 3)
    return out.reshape(1, BEAMS * CAP, 2, SUBL // 2 * LANES)


def solution(mesh):
    in_specs = (
        P("sub", "beam", None, None),
        P(None, "sub", "beam", None, None, None),
        P(None, "sub"),
        P(None, "sub", "beam", None, None),
        P(None, "sub", "beam"),
        P(None, "sub", "beam", None),
        P(None, "sub", "beam"),
        P(None, "sub", "beam"),
        P("beam", None),
    )
    out_specs = P("sub", "beam", None, None)
    return jax.shard_map(
        per_device, mesh=mesh, in_specs=in_specs, out_specs=out_specs, check_vma=False
    )
```

time: 301 us -> 215 us (0.71); the launches traced: 297 us -> 215 us
  Pallas kernels: 0 us -> 84.7 us
  blocking collectives: 55.2 us -> 0 us
  waiting for transfers between devices: 151 us -> 103 us
  other arithmetic: 31.8 us -> 7.17 us
  local copies, waits for them, and re-layouts: 26 us -> 6.46 us
  matrix products: 16 us -> 0 us
    pallas_call x0 -> x1, Pallas kernels: none -> 84.7 us  [merge_call(): pl.pallas_call(merge_kernel, out_shape=jax.ShapeDtypeStruct((BEAMS * CAP,...]
    all_to_all x1 -> x0, blocking collectives: 55.2 us -> none  [per_device(): lax.all_to_all(buffer, 'beam', split_axis=0, concat_axis=0, tiled=True)]
    ppermute x2 -> x0, waiting for transfers between devices: 45.5 us -> none  [partner_2(): return lax.ppermute(block, axis, route)]
    slice x22 -> x0, local copies, waits for them, and re-layouts: 19.8 us -> none  [the longest x19 9.84 us: interpolate(): shifted[:, :, step_size:]]
    dot_general x9 -> x0, matrix products: 16 us -> none  [the longest x2 3.22 us: project_rows(): jnp.dot(coeffs[:, 1], received_block[:, 0], precision=highest)]
    add x5 -> x2, other arithmetic: 10.6 us -> 0.08 us  [the longest x1 0.07 us: ramp_tables(): jnp.arange(8, dtype=jnp.int32)[:, None] // 2 * LANES]
    sub x3 -> x0, other arithmetic: 9.67 us -> none  [the longest x2 9.38 us: apply_ramp(): real_part = row_data[:, 0] * cos_part - row_data[:, 1] * sin_part]
    select_n x19 -> x1, other arithmetic: 10.7 us -> 4.81 us  [per_device(): got = lax.psum(jnp.where(mine, block, 0.0), 'beam')]
  transfers between devices with their start and end apart: 3 -> 1, of which waited for: 2 -> 1; matrix products, arithmetic and copies ran while one was open for 3% -> 1% of each run, Pallas kernels for 0% -> 0%
where the time goes in v1:
time: 215 us
  waiting for transfers between devices  103 us (48%)
  Pallas kernels  84.7 us (39%)
  between operations  13.5 us (6%)
  other arithmetic  7.17 us (3%)
  local copies, waits for them, and re-layouts  6.46 us (3%)
    psum x1, waiting for transfers between devices, per_device(): got = lax.psum(jnp.where(mine, block, 0.0), 'beam')  103 us
    pallas_call x1, Pallas kernels, merge_call(): pl.pallas_call(merge_kernel, out_shape=jax.ShapeDtypeStruct((BEAMS * CAP,...  84.7 us
    unnamed x17, local copies, waits for them, and re-layouts  5.88 us
    select_n x1, other arithmetic, per_device(): got = lax.psum(jnp.where(mine, block, 0.0), 'beam')  4.81 us
  transfers between devices with their start and end apart: 1, of which 1 were waited for; matrix products, arithmetic and copies ran while one was open for 1% of the time, Pallas kernels for 0%

profile of v1, /device:TPU:0, one launch (start us, length us, event | category | flops | bytes accessed | tf_op | source)
XLA Modules:
  0.0 214.5 jit_solution(3903277544676435793)
XLA Ops:
  6.5 0.0 all-reduce.2.cloned.1.call-start
  6.5 0.7 compare_bitcast_fusion
  7.2 4.8 %broadcast_select_fusion = f32[2,16,256,128]{3,2,1,0:T(8,128)} fusion(f32[2,16,256,128]{3,2,1,0:T(8,128)} %bitcast.26, pred[2]{0:T(512)(128)(4,1)S(1)} %compare_bitcast_fusion), kind=kLoop, calls=%fused_computation | loop fusion | flops 1048576 | bytes 8388610 | tf_op jit(solution)/shard_map/jit(_where)/select_n | solution.py:255
  12.0 0.0 copy-start.3
  12.0 0.0 copy-start.4
  12.0 0.0 copy-start.2
  12.0 0.0 copy-start.1
  12.0 0.0 copy-start.5
  12.0 0.0 copy-start.6
  12.0 0.0 copy-start
  12.1 0.0 all-reduce.2.cloned.1.call-update
  12.1 0.6 copy-done.3
  12.7 0.1 broadcast_multiply_fusion
  12.8 0.1 mul.78
  12.8 0.0 copy-done.4
  12.8 0.1 sine_reduce_fusion
  12.9 0.1 cos.16.turn_cos
  13.0 0.1 sin.16.turn_sin
  13.1 0.0 copy-done.2
  13.1 0.1 copy.17
  13.1 0.1 reshape_squeeze.17.taps
  13.2 0.0 copy-done.1
  13.2 0.1 reshape_squeeze.15.weights
  13.3 0.5 broadcast.126
  13.9 0.0 copy-done.5
  13.9 0.6 reduce.11
  14.5 0.1 reshape_squeeze.16.offsets
  14.6 0.0 copy-done.6
  14.6 0.2 convert_reduce_fusion.1
  14.8 0.1 convert_reduce_fusion
  14.9 0.1 iota_add_fusion
  15.0 0.6 fusion.3
  15.6 102.7 %all-reduce.2.cloned.1.call-done.got_ref = f32[2,16,256,128]{3,2,1,0:T(8,128)} async-done(((f32[2,16,256,128]{3,2,1,0:T(8,128)}), f32[2,16,256,128]{3,2,1,0:T(8,128)}) %all-reduce.2.cloned.1.call-update) | async-done | bytes 4194320 | tf_op jit(solution)/shard_map/psum | solution.py:255
  118.3 0.0 copy-done
  118.3 84.7 %shard_map.91 = f32[32,256,128]{2,1,0:T(8,128)} custom-call(f32[1024]{0:T(1024)S(1)} %reshape_squeeze.15.weights, s32[32]{0:T(128)S(1)} %reshape_squeeze.16.offsets, f32[256]{0:T(256)S(1)} %reshape_squeeze.17.taps, f32[1024]{0:T(1024)S(1)} %get-tuple-element.12.block_cos, f32[1024]{0:T(1024)S(1)} %get-tuple-element.11.block_sin, f32[32]{0:T(128)S(1)} %cos.16.turn_cos, ...), custom_call_target="tpu_custom_call" | custom-call | tf_op jit(solution)/shard_map/pallas_call | solution.py:200
  203.0 4.7 %copy.23 = f32[1,32,2,16384]{3,2,1,0:T(2,128)} copy(f32[1,32,2,16384]{3,2,1,0:T(2,128)} %bitcast.25) | data formatting | bytes 8388608
  (4 shorter events, 0.1 us)
Async XLA Ops:
  6.5 111.7 %all-reduce.2.cloned.1.call-start = ((), (), s32[]{:S(2)}) async-start(), calls=%async_computation | async-start | bytes 8388608 | tf_op jit(solution)/shard_map/psum | solution.py:255
  12.0 0.7 copy-start.3
  12.0 0.8 copy-start.4
  12.0 1.1 copy-start.2
  12.0 1.2 copy-start.1
  12.0 1.9 copy-start.5
  12.0 2.6 %copy-start.6 = (s32[16,1]{0,1:T(1,128)S(1)}, s32[16,1]{0,1:T(1,128)}, u32[]{:S(2)}) copy-start(s32[16,1]{0,1:T(1,128)} %param.17) | copy-start | bytes 196
  12.0 106.2 %copy-start = (f32[1,16,2,16384]{3,2,1,0:T(2,128)S(1)}, f32[1,16,2,16384]{3,2,1,0:T(2,128)}, u32[]{:S(2)}) copy-start(f32[1,16,2,16384]{3,2,1,0:T(2,128)} %param.9) | copy-start | bytes 6291460
Sparse Core Ops, SparseCore 0:
  12.2 106.0 all-reduce.1

commit v2 on v1

--- a/solution.py
+++ b/solution.py
@@ -3,6 +3,7 @@
 
 import jax
 import jax.numpy as jnp
+import numpy as np
 from jax import lax
 from jax.experimental import pallas as pl
 from jax.experimental.pallas import tpu as pltpu
@@ -149,30 +150,31 @@
         lax.fori_loop(1, BEAMS, send, 0)
         copy_own(c).start()
 
-    project(0, 0)
-    project(1, 0)
-    for c in range(CHUNKS):
+    def start_core(c):
         lo = c * CS
         if c + 1 < CHUNKS:
             project(0, lo + CS)
 
-        def row0(g, _, lo=lo):
+        def row0(g, _):
             first[g, pl.ds(lo, CS), :] = sub_ref[g, pl.ds(lo, CS), :] + added(0, g, lo)
             return 0
         lax.fori_loop(0, ROWS, row0, 0)
         if c == 0:
             pl.semaphore_wait(barrier, BEAMS + 1)
         copy_core(c).start()
+
+    def start_y(c):
+        lo = c * CS
         if c + 1 < CHUNKS:
             project(1, lo + CS)
 
-        def row1(g, _, lo=lo):
+        def row1(g, _):
             late[g] = added(1, g, lo)
             return 0
         lax.fori_loop(0, ROWS, row1, 0)
         copy_core(c).wait_recv()
 
-        def turn0(g, _, lo=lo):
+        def turn0(g, _):
             got = first_in[g, pl.ds(lo, CS), :]
             second[g, pl.ds(lo, CS), :] = (
                 first[g, pl.ds(lo, CS), :] + late[g]
@@ -180,8 +182,16 @@
             return 0
         lax.fori_loop(0, ROWS, turn0, 0)
         copy_y(c).start()
-        if c >= 1:
-            finish(c - 1)
+
+    project(0, 0)
+    project(1, 0)
+    start_core(0)
+    for c in range(CHUNKS):
+        if c + 1 < CHUNKS:
+            start_core(c + 1)
+        start_y(c)
+    for c in range(CHUNKS - 1):
+        finish(c)
     finish(CHUNKS - 1)
     for c in range(CHUNKS):
         copy_core(c).wait_send()
@@ -191,6 +201,115 @@
     pltpu.make_async_copy(rest, rest, beam_send).wait()
     landed = out_ref.at[pl.ds(0, (BEAMS - 1) * CAP)]
     pltpu.make_async_copy(landed, landed, beam_recv).wait()
+
+
+STEP = ((1, 0), (0, 1), (-1, 0), (0, -1))
+TREE = {
+    (0, 1): (1, 1), (0, 2): (1, 2), (0, 3): (1, 3), (1, 0): (3, 3), (1, 1): (0, 2), (1, 2): (0, 3),
+    (1, 3): (1, 4), (2, 0): (3, 4), (2, 1): (2, 3), (2, 2): (0, 4), (2, 3): (1, 5), (3, 0): (3, 3),
+    (3, 1): (2, 2), (3, 2): (1, 3), (3, 3): (1, 4),
+}
+DEPTH = 5
+PARTS = 8
+PS = SUBL // PARTS
+STEPS = PARTS + DEPTH - 1
+
+
+def tree_table():
+    arrive = {}
+    for (x, z), (way, hops) in TREE.items():
+        for r in range(4):
+            arrive[(x, z), r] = ((way + r) % 4, hops)
+            x, z = -z % 4, x
+    table = np.zeros((16, 12), np.int32)
+    for x in range(4):
+        for z in range(4):
+            for e in range(4):
+                there = ((x + STEP[e][0]) % 4, (z + STEP[e][1]) % 4)
+                for r in range(4):
+                    if (x, z) != (0, 0) and there != (0, 0) and arrive[there, r][0] == e:
+                        table[x * 4 + z, e] = arrive[(x, z), r][0]
+            for r in range(4):
+                if (x, z) != (0, 0):
+                    table[x * 4 + z, 4 + r] = arrive[(x, z), r][0]
+                    table[x * 4 + z, 8 + r] = arrive[(x, z), r][1] - 1
+    return table.reshape(-1)
+
+
+def ingest_kernel(owner, table, block_ref, got_ref, *scratch):
+    landing = [scratch[s * STEPS : (s + 1) * STEPS] for s in range(2)]
+    stage, send_sem, recv_sem = scratch[2 * STEPS :]
+    sub = lax.axis_index("sub")
+    me = lax.axis_index("beam")
+    x, z = me // 4, me % 4
+    peers = [(sub, (x + dx + 4) % 4 * 4 + (z + dz + 4) % 4) for dx, dz in STEP]
+    barrier = pltpu.get_barrier_semaphore()
+    for peer in peers:
+        pl.semaphore_signal(barrier, inc=1, device_id=peer, device_id_type=MESH)
+    place = []
+    for s in range(2):
+        o = owner[s]
+        place.append((((x - o // 4) & 3) * 4 + ((z - o % 4) & 3)) * 12)
+    root = [place[s] == 0 for s in range(2)]
+    pl.semaphore_wait(barrier, 4)
+
+    for t in range(STEPS):
+        for s in range(2):
+            if t > 0:
+                last = landing[s][t - 1]
+                pltpu.make_async_copy(last, last, recv_sem.at[s, t - 1]).wait()
+            for e in range(4):
+                q = (e + 3) % 4
+                if t < PARTS:
+                    own = block_ref.at[s, pl.ds(4 * q, 4), pl.ds(t * PS, PS), :]
+                if t == 0:
+                    source = own
+                else:
+                    value = last[table[place[s] + e]]
+                    if t < PARTS:
+                        value = jnp.where(root[s], own[...], value)
+                    source = stage.at[s, t - 1, e]
+                    source[...] = value
+                pltpu.make_async_remote_copy(
+                    src_ref=source, dst_ref=landing[s][t].at[e], send_sem=send_sem, recv_sem=recv_sem.at[s, t],
+                    device_id=peers[e], device_id_type=MESH).start()
+    for s in range(2):
+        last = landing[s][STEPS - 1]
+        pltpu.make_async_copy(last, last, recv_sem.at[s, STEPS - 1]).wait()
+    for s in range(2):
+        for r in range(4):
+            way = table[place[s] + 4 + r]
+            late = table[place[s] + 8 + r]
+            for c in range(PARTS):
+                own = block_ref[s, pl.ds(4 * r, 4), pl.ds(c * PS, PS), :]
+                value = landing[s][c][way]
+                for d in range(1, DEPTH):
+                    value = jnp.where(late == d, landing[s][c + d][way], value)
+                got_ref[s, pl.ds(4 * r, 4), pl.ds(c * PS, PS), :] = jnp.where(root[s], own, value)
+    for s in range(2):
+        own = block_ref.at[s, :, pl.ds(0, PS), :]
+        pltpu.make_async_copy(own, own, send_sem).wait()
+        pltpu.make_async_copy(stage.at[s], stage.at[s], send_sem).wait()
+
+
+def ingest(owner, blocks):
+    smem = pl.BlockSpec(memory_space=pltpu.SMEM)
+    vmem = pl.BlockSpec(memory_space=pltpu.VMEM)
+    part = pltpu.VMEM((4, 4, PS, LANES), jnp.float32)
+    return pl.pallas_call(
+        ingest_kernel,
+        out_shape=jax.ShapeDtypeStruct((2, PB, SUBL, LANES), jnp.float32),
+        in_specs=[smem, smem, vmem],
+        out_specs=vmem,
+        scratch_shapes=[part] * (2 * STEPS) + [
+            pltpu.VMEM((2, STEPS - 1, 4, 4, PS, LANES), jnp.float32),
+            pltpu.SemaphoreType.DMA,
+            pltpu.SemaphoreType.DMA((2, STEPS)),
+        ],
+        compiler_params=pltpu.CompilerParams(
+            collective_id=2, has_side_effects=True, vmem_limit_bytes=32 * 2**20
+        ),
+    )(owner, jnp.asarray(tree_table()), blocks)
 
 
 def merge_call(scalars, rows, got, cos_table, sin_table):
@@ -249,10 +368,7 @@
 def per_device(
     subimage, pulses, ingest_owner, weights, offsets, filter_taps, cycles, merge_phase, destination
 ):
-    me = lax.axis_index("beam")
-    mine = (ingest_owner[:, 0] == me)[:, None, None, None]
-    block = paired(pulses[:, 0, 0])
-    got = lax.psum(jnp.where(mine, block, 0.0), "beam")
+    got = ingest(ingest_owner[:, 0], paired(pulses[:, 0, 0]))
     coarse_cos, coarse_sin, fine_cos, fine_sin = ramp_tables(cycles[:, 0])
     targets = destination[:, 0]
     same_owner = targets[:, None] == targets[None, :]

time: 215 us -> 185 us (0.86)
  waiting for transfers between devices: 103 us -> 0 us
  Pallas kernels: 84.7 us -> 166 us
  between operations: 13.5 us -> 0.06 us
  local copies, waits for them, and re-layouts: 6.46 us -> 13.5 us
    psum x1 -> x0, waiting for transfers between devices: 103 us -> none  [per_device(): got = lax.psum(jnp.where(mine, block, 0.0), 'beam')]
    pallas_call x0 -> x1, Pallas kernels: none -> 57.4 us  [ingest(): pl.pallas_call(ingest_kernel, out_shape=jax.ShapeDtypeStruct((2, PB, SUBL...]
    pallas_call x1, Pallas kernels: 84.7 us -> 108 us  [merge_call(): pl.pallas_call(merge_kernel, out_shape=jax.ShapeDtypeStruct((BEAMS * CAP,...]
    unnamed x17 -> x13, local copies, waits for them, and re-layouts: 5.88 us -> 11.5 us
    select_n x1 -> x0, other arithmetic: 4.81 us -> none  [per_device(): got = lax.psum(jnp.where(mine, block, 0.0), 'beam')]
  transfers between devices with their start and end apart: 1 -> 0, of which waited for: 1 -> 0; matrix products, arithmetic and copies ran while one was open for 1% -> 0% of each run, Pallas kernels for 0% -> 0%
where the time goes in v2:
time: 185 us; the launch traced here: 184 us
  Pallas kernels  166 us (90%)
  local copies, waits for them, and re-layouts  13.5 us (7%)
  other arithmetic  5.15 us (3%)
    pallas_call x1, Pallas kernels, merge_call(): pl.pallas_call(merge_kernel, out_shape=jax.ShapeDtypeStruct((BEAMS * CAP,...  108 us
    pallas_call x1, Pallas kernels, ingest(): pl.pallas_call(ingest_kernel, out_shape=jax.ShapeDtypeStruct((2, PB, SUBL...  57.4 us
    unnamed x13, local copies, waits for them, and re-layouts  11.5 us

profile of v2, /device:TPU:0, one launch (start us, length us, event | category | flops | bytes accessed | tf_op | source)
XLA Modules:
  0.0 184.5 jit_solution(10112536531099800745)
XLA Ops:
  0.0 0.5 broadcast.120
  0.5 1.3 reduce.11
  1.9 0.1 reshape_squeeze.16.offsets
  1.9 0.9 convert_reduce_fusion.1
  2.9 0.7 multiply_add_fusion
  3.5 0.1 convert_reduce_fusion
  3.6 0.7 sine_reduce_fusion
  4.3 0.1 sin.16.turn_sin
  4.4 0.1 cos.16.turn_cos
  4.5 0.1 iota_add_fusion
  4.6 0.9 reshape_squeeze.15.weights
  5.4 0.8 broadcast_multiply_fusion
  6.2 0.1 mul.78
  6.3 0.1 fusion.9
  6.3 0.8 copy.18
  7.1 0.1 reshape_squeeze.17.taps
  7.2 1.3 fusion.3
  8.5 0.0 copy-start.1
  8.5 2.2 %copy-done.1 = f32[2,1,1,16,2,16384]{5,4,3,2,1,0:T(2,128)S(1)} copy-done((f32[2,1,1,16,2,16384]{5,4,3,2,1,0:T(2,128)S(1)}, f32[2,1,1,16,2,16384]{5,4,3,2,1,0:T(2,128)}, u32[]{:S(2)}) %copy-start.1) | copy-done | bytes 4194328
  10.7 0.0 copy-start.3
  10.7 0.7 copy-done.3
  11.3 0.0 copy-start.4
  11.3 0.7 copy-done.4
  12.0 0.0 copy-start.2
  12.0 57.4 %shard_map.100.got_ref = f32[2,16,256,128]{3,2,1,0:T(8,128)S(1)} custom-call(s32[2]{0:T(128)S(1)} %bitcast.25, s32[192]{0:T(256)S(1)} %copy-done.3, f32[2,16,256,128]{3,2,1,0:T(8,128)S(1)} %bitcast.23), custom_call_target="tpu_custom_call" | custom-call | tf_op jit(solution)/shard_map/pallas_call | solution.py:299
  69.4 0.0 copy-start
  69.4 2.0 %copy-done = f32[2,16,256,128]{3,2,1,0:T(8,128)} copy-done((f32[2,16,256,128]{3,2,1,0:T(8,128)}, f32[2,16,256,128]{3,2,1,0:T(8,128)S(1)}, u32[]{:S(2)}) %copy-start) | copy-done | bytes 4194328
  71.4 0.0 copy-done.2
  71.4 108.4 %shard_map.101 = f32[32,256,128]{2,1,0:T(8,128)} custom-call(f32[1024]{0:T(1024)S(1)} %reshape_squeeze.15.weights, s32[32]{0:T(128)S(1)} %reshape_squeeze.16.offsets, f32[256]{0:T(256)S(1)} %reshape_squeeze.17.taps, f32[1024]{0:T(1024)S(1)} %get-tuple-element.12.block_cos, f32[1024]{0:T(1024)S(1)} %get-tuple-element.11.block_sin, f32[32]{0:T(128)S(1)} %cos.16.turn_cos, ...), custom_call_target="tpu_custom_call" | custom-call | tf_op jit(solution)/shard_map/pallas_call | solution.py:319
  179.8 4.7 %copy.23 = f32[1,32,2,16384]{3,2,1,0:T(2,128)} copy(f32[1,32,2,16384]{3,2,1,0:T(2,128)} %bitcast.26) | data formatting | bytes 8388608
  (2 shorter events, 0.0 us)
Async XLA Ops:
  8.5 2.2 %copy-start.1 = (f32[2,1,1,16,2,16384]{5,4,3,2,1,0:T(2,128)S(1)}, f32[2,1,1,16,2,16384]{5,4,3,2,1,0:T(2,128)}, u32[]{:S(2)}) copy-start(f32[2,1,1,16,2,16384]{5,4,3,2,1,0:T(2,128)} %param.11) | copy-start | bytes 12582916
  10.7 0.7 copy-start.3
  11.3 0.7 copy-start.4
  12.0 59.4 %copy-start.2 = (f32[1,16,2,16384]{3,2,1,0:T(2,128)S(1)}, f32[1,16,2,16384]{3,2,1,0:T(2,128)}, u32[]{:S(2)}) copy-start(f32[1,16,2,16384]{3,2,1,0:T(2,128)} %param.10) | copy-start | bytes 6291460
  69.4 2.0 %copy-start = (f32[2,16,256,128]{3,2,1,0:T(8,128)}, f32[2,16,256,128]{3,2,1,0:T(8,128)S(1)}, u32[]{:S(2)}) copy-start(f32[2,16,256,128]{3,2,1,0:T(8,128)S(1)} %shard_map.100.got_ref) | copy-start | bytes 12582916

commit v3 on v0

v3 whole, which is shorter than its diff:
```python
import math

import jax
import jax.numpy as jnp
import numpy as np
from jax import lax
from jax.experimental import pallas as pl
from jax.experimental.pallas import tpu as pltpu
from jax.sharding import PartitionSpec as P

CAP = 2
TAPS = 8
PB = 16
ROWS = 16
BEAMS = 16
SLOTS = BEAMS * CAP
LANES = 128
LENGTH = 16384
SUBL = 256
PAD = 32
MESH = pl.DeviceIdType.MESH

STEP = ((1, 0), (0, 1), (-1, 0), (0, -1))
TREE = {
    (0, 1): (1, 1), (0, 2): (1, 2), (0, 3): (1, 3), (1, 0): (3, 3), (1, 1): (0, 2), (1, 2): (0, 3),
    (1, 3): (1, 4), (2, 0): (3, 4), (2, 1): (2, 3), (2, 2): (0, 4), (2, 3): (1, 5), (3, 0): (3, 3),
    (3, 1): (2, 2), (3, 2): (1, 3), (3, 3): (1, 4),
}
DEPTH = 5
PARTS = 8
PS = SUBL // PARTS
STEPS = PARTS + DEPTH - 1
HALO = 16
BOUNDS = [0] + [PS * i - HALO for i in range(1, PARTS + 1)] + [SUBL]
CHUNKS = PARTS + 1
WINDOW = 2


def tree_table():
    arrive = {}
    for (x, z), (way, hops) in TREE.items():
        for r in range(4):
            arrive[(x, z), r] = ((way + r) % 4, hops)
            x, z = -z % 4, x
    table = np.zeros((16, 12), np.int32)
    for x in range(4):
        for z in range(4):
            for e in range(4):
                there = ((x + STEP[e][0]) % 4, (z + STEP[e][1]) % 4)
                for r in range(4):
                    if (x, z) != (0, 0) and there != (0, 0) and arrive[there, r][0] == e:
                        table[x * 4 + z, e] = arrive[(x, z), r][0]
            for r in range(4):
                if (x, z) != (0, 0):
                    table[x * 4 + z, 4 + r] = arrive[(x, z), r][0]
                    table[x * 4 + z, 8 + r] = arrive[(x, z), r][1] - 1
    return table.reshape(-1)


def swapped(x):
    shape = x.shape
    y = x.reshape(-1, 8, LANES)
    even = lax.broadcasted_iota(jnp.int32, y.shape, 1) % 2 == 0
    return jnp.where(even, pltpu.roll(y, 7, 1), pltpu.roll(y, 1, 1)).reshape(shape)


def pair_sign(rows):
    even = lax.broadcasted_iota(jnp.int32, (rows, LANES), 0) % 2 == 0
    return jnp.where(even, -1.0, 1.0).astype(jnp.float32)


def turn(n):
    quarter = (n + LENGTH // 8) // (LENGTH // 4)
    x = (n - quarter * (LENGTH // 4)).astype(jnp.float32) * (2.0 * math.pi / LENGTH)
    q = x * x
    c = 1.0 + q * (-1.0 / 2 + q * (1.0 / 24 + q * (-1.0 / 720 + q * (1.0 / 40320))))
    s = x * (1.0 + q * (-1.0 / 6 + q * (1.0 / 120 + q * (-1.0 / 5040 + q * (1.0 / 362880)))))
    odd = quarter % 2 == 1
    half = quarter % 4
    cos = jnp.where(odd, s, c) * jnp.where((half == 1) | (half == 2), -1.0, 1.0)
    sin = jnp.where(odd, c, s) * jnp.where(half >= 2, -1.0, 1.0)
    return cos, sin


def kernel(
    owner, weights, offsets, taps, cycles, phases, targets, table,
    sub_hbm, pulse_hbm,
    out_ref,
    *scratch,
):
    landing = [scratch[s * STEPS : (s + 1) * STEPS] for s in range(2)]
    (stage, sub_ref, block_ref, got, got_turned, proj, shifted, ramped, ramp_cos, ramp_sin, step_cos, step_sin,
     turn_cos, turn_sin, first, first_in, second, second_in, merged, slots, slot_row,
     load_sem, part_send, part_recv, core_send, core_recv, y_send, y_recv, beam_send, beam_recv, own_sem,
     ) = scratch[2 * STEPS :]
    sub = lax.axis_index("sub")
    me = lax.axis_index("beam")
    x, z = me // 4, me % 4
    core_peer = (sub ^ 1, me)
    y_peer = (sub ^ 2, me)
    peers = [(sub, (x + dx + 4) % 4 * 4 + (z + dz + 4) % 4) for dx, dz in STEP]

    barrier = pltpu.get_barrier_semaphore()
    pl.semaphore_signal(barrier, inc=1, device_id=core_peer, device_id_type=MESH)
    pl.semaphore_signal(barrier, inc=1, device_id=y_peer, device_id_type=MESH)
    for shift in range(1, BEAMS):
        pl.semaphore_signal(barrier, inc=1, device_id=(sub, me ^ shift), device_id_type=MESH)

    loads = [pltpu.make_async_copy(pulse_hbm, block_ref, load_sem.at[0]),
             pltpu.make_async_copy(sub_hbm, sub_ref, load_sem.at[1])]
    for load in loads:
        load.start()

    place = []
    for s in range(2):
        o = owner[s, 0]
        place.append((((x - o // 4) & 3) * 4 + ((z - o % 4) & 3)) * 12)
    root = [place[s] == 0 for s in range(2)]

    def prepare_rows(s, lo, hi):
        sublane = lax.broadcasted_iota(jnp.int32, (8, LANES), 0)
        place_in = sublane // 2 * LANES + lax.broadcasted_iota(jnp.int32, (8, LANES), 1)
        sign = pair_sign(8)

        def prepare(g, _):
            count = cycles[s, 0, g]
            cos, sin = turn((place_in * count) % LENGTH)
            ramp_cos[s, g] = cos
            ramp_sin[s, g] = sin * sign
            whole = jnp.full((8, LANES), (count * (4 * LANES)) % LENGTH, jnp.int32)
            cos, sin = turn(whole)
            step_cos[s, g] = cos
            step_sin[s, g] = sin * sign
            phase = jnp.full((8, LANES), phases[s, 0, g], jnp.float32)
            turn_cos[s, g] = jnp.cos(phase)
            turn_sin[s, g] = jnp.sin(phase) * sign
            return 0
        lax.fori_loop(lo, hi, prepare, 0)

    def prepare_slots():
        def one(o, _):
            low, high = jnp.int32(ROWS), jnp.int32(ROWS)
            for g in reversed(range(ROWS)):
                hit = targets[g, 0] == o
                high = jnp.where(hit, low, high)
                low = jnp.where(hit, g, low)
            slot_row[CAP * o] = low
            slot_row[CAP * o + 1] = high
            return 0
        lax.fori_loop(0, BEAMS, one, 0)

        def clear(g, _):
            for s in range(2):
                proj[s, g, pl.ds(SUBL, PAD), :] = jnp.zeros((PAD, LANES), jnp.float32)
            return 0
        lax.fori_loop(0, ROWS, clear, 0)

    def forward(s, t):
        if t > 0:
            last = landing[s][t - 1]
            pltpu.make_async_copy(last, last, part_recv.at[s, t - 1]).wait()
        if t == STEPS:
            return
        for e in range(4):
            q = (e + 3) % 4
            if t < PARTS:
                own = block_ref.at[s, pl.ds(4 * q, 4), pl.ds(t * PS, PS), :]
            if t == 0:
                source = own
            else:
                value = last[table[place[s] + e]]
                if t < PARTS:
                    value = jnp.where(root[s], own[...], value)
                source = stage.at[s, t - 1, e]
                source[...] = value
            pltpu.make_async_remote_copy(
                src_ref=source, dst_ref=landing[s][t].at[e], send_sem=part_send, recv_sem=part_recv.at[s, t],
                device_id=peers[e], device_id_type=MESH).start()

    def assemble(s, c):
        for r in range(4):
            way = table[place[s] + 4 + r]
            late = table[place[s] + 8 + r]
            for p in range(4):
                own = block_ref[s, 4 * r + p, pl.ds(c * PS, PS), :]
                value = landing[s][c][way, p]
                for d in range(1, DEPTH):
                    value = jnp.where(late == d, landing[s][c + d][way, p], value)
                value = jnp.where(root[s], own, value)
                got[4 * r + p] = value
                got_turned[4 * r + p] = swapped(value) * pair_sign(PS)

    def project(s, c):
        def half(h, _):
            acc = [None] * 8
            for p in range(PB):
                b = got[p]
                t = got_turned[p]
                for k in range(8):
                    g = h * 8 + k
                    term = weights[s, 0, g, 0, p] * b + weights[s, 0, g, 1, p] * t
                    acc[k] = term if acc[k] is None else acc[k] + term
            for k in range(8):
                g = h * 8 + k
                off = offsets[s, 0, g] % LANES
                proj[s, g, pl.ds(c * PS, PS), :] = pltpu.roll(acc[k], (LANES - off) % LANES, 1)
            return 0
        lax.fori_loop(0, 2, half, 0)

    def added(s, g, k):
        lo, n = BOUNDS[k], BOUNDS[k + 1] - BOUNDS[k]
        wide = n + 8
        lane = lax.broadcasted_iota(jnp.int32, (wide, LANES), 1)
        off = offsets[s, 0, g]
        start = lo + 2 * (off // LANES)
        inside = lane < LANES - off % LANES
        u0 = proj[s, g, pl.ds(start, wide), :]
        u1 = proj[s, g, pl.ds(start + 2, wide), :]
        u2 = proj[s, g, pl.ds(start + 4, wide), :]
        here = jnp.where(inside, u0, u1)
        following = jnp.where(inside, u1, u2)
        moved = [here]
        for i in range(1, 4):
            moved.append(pltpu.roll(jnp.where(lane < i, following, here), LANES - i, 1))
        near = taps[s, 0, g, 0] * here[:n]
        far = taps[s, 0, g, 4] * here
        for i in range(1, 4):
            near = near + taps[s, 0, g, i] * moved[i][:n]
            far = far + taps[s, 0, g, 4 + i] * moved[i]
        shifted[g, pl.ds(0, wide), :] = far
        beyond = shifted[g, pl.ds(2, n), :]
        acc = near + pltpu.roll(jnp.where(lane[:n] < 4, beyond, far[:n]), LANES - 4, 1)
        ramped[g, pl.ds(8, n), :] = acc
        even = lax.broadcasted_iota(jnp.int32, (n, LANES), 0) % 2 == 0
        turned = jnp.where(even, ramped[g, pl.ds(9, n), :], ramped[g, pl.ds(7, n), :])
        cos, sin = ramp_cos[s, g], ramp_sin[s, g]
        cos_by, sin_by = step_cos[s, g], step_sin[s, g]
        parts = []
        for v in range(n // 8):
            parts.append(acc[v * 8 : v * 8 + 8] * cos + turned[v * 8 : v * 8 + 8] * sin)
            cos, sin = cos * cos_by - sin * sin_by, sin * cos_by + cos * sin_by
        ramp_cos[s, g] = cos
        ramp_sin[s, g] = sin
        return jnp.concatenate(parts, axis=0)

    def span(k):
        return pl.ds(BOUNDS[k], BOUNDS[k + 1] - BOUNDS[k])

    def copy_core(k):
        return pltpu.make_async_remote_copy(
            src_ref=first.at[:, span(k), :], dst_ref=first_in.at[:, span(k), :],
            send_sem=core_send.at[k], recv_sem=core_recv.at[k], device_id=core_peer, device_id_type=MESH)

    def copy_y(k):
        return pltpu.make_async_remote_copy(
            src_ref=second.at[:, span(k), :], dst_ref=second_in.at[:, span(k), :],
            send_sem=y_send.at[k], recv_sem=y_recv.at[k], device_id=y_peer, device_id_type=MESH)

    def copy_own(k):
        return pltpu.make_async_copy(
            slots.at[pl.ds(me * CAP, CAP), span(k), :], out_ref.at[pl.ds(me * CAP, CAP), span(k), :], own_sem.at[k])

    def rotated(value, s, g):
        n = value.shape[0] // 8
        y = value.reshape(n, 8, LANES)
        t = swapped(value).reshape(n, 8, LANES)
        return (y * turn_cos[s, g][None] + t * turn_sin[s, g][None]).reshape(value.shape)

    def begin(k):
        def row0(g, _):
            first[g, span(k), :] = sub_ref[g, span(k), :] + added(0, g, k)
            return 0
        lax.fori_loop(0, ROWS, row0, 0, unroll=4)
        copy_core(k).start()

    def extend(k):
        def row1(g, _):
            second[g, span(k), :] = first[g, span(k), :] + added(1, g, k)
            return 0
        lax.fori_loop(0, ROWS, row1, 0, unroll=4)

    def meet(k):
        copy_core(k).wait_recv()

        def row(g, _):
            second[g, span(k), :] = second[g, span(k), :] + rotated(first_in[g, span(k), :], 0, g)
            return 0
        lax.fori_loop(0, ROWS, row, 0, unroll=4)

    def finish(k):
        copy_y(k).wait_recv()
        if k + WINDOW < CHUNKS:
            copy_y(k + WINDOW).start()
        n = BOUNDS[k + 1] - BOUNDS[k]

        def row(g, _):
            merged[g, pl.ds(0, n), :] = second[g, span(k), :] + rotated(second_in[g, span(k), :], 1, g)
            return 0
        lax.fori_loop(0, ROWS, row, 0, unroll=4)

        def slot(q, _):
            g = slot_row[q]
            value = merged[jnp.minimum(g, ROWS - 1), pl.ds(0, n), :]
            slots[q, span(k), :] = jnp.where(g < ROWS, value, 0.0)
            return 0
        lax.fori_loop(0, SLOTS, slot, 0, unroll=8)

        def send(shift, _):
            to = me ^ shift
            pltpu.make_async_remote_copy(
                src_ref=slots.at[pl.ds(to * CAP, CAP), span(k), :],
                dst_ref=out_ref.at[pl.ds(me * CAP, CAP), span(k), :],
                send_sem=beam_send, recv_sem=beam_recv, device_id=(sub, to), device_id_type=MESH).start()
            return 0
        lax.fori_loop(1, BEAMS, send, 0)
        copy_own(k).start()

    pl.semaphore_wait(barrier, BEAMS + 1)
    for load in loads:
        load.wait()
    for t in range(STEPS + 1):
        for s in range(2):
            forward(s, t)
        if t < 4:
            prepare_rows(t // 2, t % 2 * 8, t % 2 * 8 + 8)
        if t == 4:
            prepare_slots()
        c = t - DEPTH
        if c >= 1:
            meet(c - 1)
            if c - 1 < WINDOW:
                copy_y(c - 1).start()
        if c >= 0:
            assemble(0, c)
            project(0, c)
            begin(c)
            assemble(1, c)
            project(1, c)
            extend(c)
    begin(CHUNKS - 1)
    extend(CHUNKS - 1)
    meet(CHUNKS - 2)
    meet(CHUNKS - 1)
    for k in range(CHUNKS):
        finish(k)

    for s in range(2):
        own = block_ref.at[s, :, pl.ds(0, PS), :]
        pltpu.make_async_copy(own, own, part_send).wait()
        pltpu.make_async_copy(stage.at[s], stage.at[s], part_send).wait()
    for k in range(CHUNKS):
        copy_core(k).wait_send()
        copy_y(k).wait_send()
        copy_own(k).wait()
    rest = slots.at[pl.ds(0, SLOTS - CAP)]
    pltpu.make_async_copy(rest, rest, beam_send).wait()
    landed = out_ref.at[pl.ds(0, SLOTS - CAP)]
    pltpu.make_async_copy(landed, landed, beam_recv).wait()


def call(*operands):
    smem = pl.BlockSpec(memory_space=pltpu.SMEM)
    hbm = pl.BlockSpec(memory_space=pl.ANY)

    def vmem(*shape):
        return pltpu.VMEM((*shape, LANES), jnp.float32)

    return pl.pallas_call(
        kernel,
        out_shape=jax.ShapeDtypeStruct((SLOTS, SUBL, LANES), jnp.float32),
        in_specs=[smem] * 8 + [hbm] * 2,
        out_specs=hbm,
        scratch_shapes=[vmem(4, 4, PS)] * (2 * STEPS) + [
            vmem(2, STEPS - 1, 4, 4, PS),
            vmem(ROWS, SUBL),
            vmem(2, PB, SUBL),
            vmem(PB, PS),
            vmem(PB, PS),
            vmem(2, ROWS, SUBL + PAD),
            vmem(ROWS, PS + 8),
            vmem(ROWS, PS + 16),
            vmem(2, ROWS, 8),
            vmem(2, ROWS, 8),
            vmem(2, ROWS, 8),
            vmem(2, ROWS, 8),
            vmem(2, ROWS, 8),
            vmem(2, ROWS, 8),
            vmem(ROWS, SUBL),
            vmem(ROWS, SUBL),
            vmem(ROWS, SUBL),
            vmem(ROWS, SUBL),
            vmem(ROWS, PS),
            vmem(SLOTS, SUBL),
            pltpu.SMEM((SLOTS,), jnp.int32),
            pltpu.SemaphoreType.DMA((2,)),
            pltpu.SemaphoreType.DMA,
            pltpu.SemaphoreType.DMA((2, STEPS)),
            pltpu.SemaphoreType.DMA((CHUNKS,)),
            pltpu.SemaphoreType.DMA((CHUNKS,)),
            pltpu.SemaphoreType.DMA((CHUNKS,)),
            pltpu.SemaphoreType.DMA((CHUNKS,)),
            pltpu.SemaphoreType.DMA,
            pltpu.SemaphoreType.DMA,
            pltpu.SemaphoreType.DMA((CHUNKS,)),
        ],
        compiler_params=pltpu.CompilerParams(
            collective_id=1, has_side_effects=True, vmem_limit_bytes=56 * 2**20
        ),
    )(*operands)


def paired(x):
    lead = x.shape[:-2]
    n = len(lead)
    y = x.reshape(*lead, 2, SUBL // 2, LANES)
    y = y.transpose(*range(n), n + 1, n, n + 2)
    return y.reshape(*lead, SUBL, LANES)


def per_device(
    subimage, pulses, ingest_owner, weights, offsets, filter_taps, cycles, merge_phase, destination
):
    out = call(
        ingest_owner, weights, offsets, filter_taps, cycles, merge_phase, destination, jnp.asarray(tree_table()),
        paired(subimage[0]), paired(pulses[:, 0, 0]),
    )
    out = out.reshape(SLOTS, SUBL // 2, 2, LANES).transpose(0, 2, 1, 3)
    return out.reshape(1, SLOTS, 2, LENGTH)


def solution(mesh):
    in_specs = (
        P("sub", "beam", None, None),
        P(None, "sub", "beam", None, None, None),
        P(None, "sub"),
        P(None, "sub", "beam", None, None),
        P(None, "sub", "beam"),
        P(None, "sub", "beam", None),
        P(None, "sub", "beam"),
        P(None, "sub", "beam"),
        P("beam", None),
    )
    out_specs = P("sub", "beam", None, None)
    return jax.shard_map(
        per_device, mesh=mesh, in_specs=in_specs, out_specs=out_specs, check_vma=False
    )
```

time: 301 us -> 126 us (0.42); the launches traced: 297 us -> 126 us
  waiting for transfers between devices: 151 us -> 0 us
  Pallas kernels: 0 us -> 117 us
  blocking collectives: 55.2 us -> 0 us
  other arithmetic: 31.8 us -> 0 us
  local copies, waits for them, and re-layouts: 26 us -> 8.63 us
  matrix products: 16 us -> 0 us
  between operations: 15.4 us -> 0.01 us
    pallas_call x0 -> x1, Pallas kernels: none -> 117 us  [call(): pl.pallas_call(kernel, out_shape=jax.ShapeDtypeStruct((SLOTS, SUBL, LANES...]
    psum x1 -> x0, waiting for transfers between devices: 106 us -> none  [broadcast(): return lax.psum(block, axis)]
    all_to_all x1 -> x0, blocking collectives: 55.2 us -> none  [per_device(): lax.all_to_all(buffer, 'beam', split_axis=0, concat_axis=0, tiled=True)]
    ppermute x2 -> x0, waiting for transfers between devices: 45.5 us -> none  [partner_2(): return lax.ppermute(block, axis, route)]
    slice x22 -> x0, local copies, waits for them, and re-layouts: 19.8 us -> none  [the longest x19 9.84 us: interpolate(): shifted[:, :, step_size:]]
    dot_general x9 -> x0, matrix products: 16 us -> none  [the longest x2 3.22 us: project_rows(): jnp.dot(coeffs[:, 1], received_block[:, 0], precision=highest)]
    select_n x19 -> x0, other arithmetic: 10.7 us -> none  [the longest x1 5.37 us: broadcast(): jnp.where(lax.axis_index(axis) == holder, block, jnp.zeros_like(block))]
    add x5 -> x0, other arithmetic: 10.6 us -> none  [the longest x2 7.94 us: interpolate(): summed + filters[:, tap_index, None, None] * shifted[:, :, tap_index:tap_...]
  transfers between devices with their start and end apart: 3 -> 0, of which waited for: 2 -> 0; matrix products, arithmetic and copies ran while one was open for 3% -> 0% of each run, Pallas kernels for 0% -> 0%
where the time goes in v3:
time: 126 us
  Pallas kernels  117 us (93%)
  local copies, waits for them, and re-layouts  8.63 us (7%)
    pallas_call x1, Pallas kernels, call(): pl.pallas_call(kernel, out_shape=jax.ShapeDtypeStruct((SLOTS, SUBL, LANES...  117 us
    unnamed x4, local copies, waits for them, and re-layouts  8.63 us

profile of v3, /device:TPU:0, one launch (start us, length us, event | category | flops | bytes accessed | tf_op | source)
XLA Modules:
  0.0 125.5 jit_solution(5271449026142725654)
XLA Ops:
  0.0 1.3 %copy.13.owner = s32[2,1]{1,0:T(2,128)} copy(s32[2,1]{0,1:T(1,128)} %param.12) | data formatting | bytes 16 | tf_op args[2]
  1.3 1.3 %copy.15.targets = s32[16,1]{1,0:T(8,128)} copy(s32[16,1]{0,1:T(1,128)} %param.18) | data formatting | bytes 128 | tf_op args[8]
  2.6 1.4 %copy.14.taps = f32[2,1,16,8]{3,2,1,0:T(8,128)} copy(f32[2,1,16,8]{2,3,1,0:T(8,128)} %param.15) | data formatting | bytes 2048 | tf_op args[5]
  4.0 116.9 %shard_map.100 = f32[32,256,128]{2,1,0:T(8,128)} custom-call(s32[2,1]{1,0:T(2,128)} %copy.13.owner, f32[2,1,16,2,16]{4,3,2,1,0:T(2,128)} %weights.1, s32[2,1,16]{2,1,0:T(1,128)} %offsets.1, f32[2,1,16,8]{3,2,1,0:T(8,128)} %copy.14.taps, s32[2,1,16]{2,1,0:T(1,128)} %cycles.1, f32[2,1,16]{2,1,0:T(1,128)} %phases.1, s32[16,1]{1,0:T(8,128)} %copy.15.targets, ...), custom_call_target="tpu_custom_call" | custom-call | tf_op jit(solution)/shard_map/pallas_call | solution.py:368
  120.8 4.7 %copy.18 = f32[1,32,2,16384]{3,2,1,0:T(2,128)} copy(f32[1,32,2,16384]{3,2,1,0:T(2,128)} %bitcast.15) | data formatting | bytes 8388608

commit v4 on v3

--- a/solution.py
+++ b/solution.py
@@ -1,3 +1,4 @@
+import functools
 import math
 
 import jax
@@ -29,11 +30,12 @@
 DEPTH = 5
 PARTS = 8
 PS = SUBL // PARTS
+LINES = 4
+LP = 4 // LINES
 STEPS = PARTS + DEPTH - 1
 HALO = 16
 BOUNDS = [0] + [PS * i - HALO for i in range(1, PARTS + 1)] + [SUBL]
 CHUNKS = PARTS + 1
-WINDOW = 2
 
 
 def tree_table():
@@ -88,11 +90,11 @@
     out_ref,
     *scratch,
 ):
-    landing = [scratch[s * STEPS : (s + 1) * STEPS] for s in range(2)]
+    landing = [[scratch[(s * LINES + w) * STEPS : (s * LINES + w + 1) * STEPS] for w in range(LINES)] for s in range(2)]
     (stage, sub_ref, block_ref, got, got_turned, proj, shifted, ramped, ramp_cos, ramp_sin, step_cos, step_sin,
      turn_cos, turn_sin, first, first_in, second, second_in, merged, slots, slot_row,
      load_sem, part_send, part_recv, core_send, core_recv, y_send, y_recv, beam_send, beam_recv, own_sem,
-     ) = scratch[2 * STEPS :]
+     ) = scratch[2 * LINES * STEPS :]
     sub = lax.axis_index("sub")
     me = lax.axis_index("beam")
     x, z = me // 4, me % 4
@@ -113,7 +115,7 @@
 
     place = []
     for s in range(2):
-        o = owner[s, 0]
+        o = owner[s]
         place.append((((x - o // 4) & 3) * 4 + ((z - o % 4) & 3)) * 12)
     root = [place[s] == 0 for s in range(2)]
 
@@ -141,7 +143,7 @@
         def one(o, _):
             low, high = jnp.int32(ROWS), jnp.int32(ROWS)
             for g in reversed(range(ROWS)):
-                hit = targets[g, 0] == o
+                hit = targets[g] == o
                 high = jnp.where(hit, low, high)
                 low = jnp.where(hit, g, low)
             slot_row[CAP * o] = low
@@ -155,26 +157,26 @@
             return 0
         lax.fori_loop(0, ROWS, clear, 0)
 
-    def forward(s, t):
+    def forward(s, w, t):
         if t > 0:
-            last = landing[s][t - 1]
-            pltpu.make_async_copy(last, last, part_recv.at[s, t - 1]).wait()
+            last = landing[s][w][t - 1]
+            pltpu.make_async_copy(last, last, part_recv.at[s, w, t - 1]).wait()
         if t == STEPS:
             return
         for e in range(4):
             q = (e + 3) % 4
             if t < PARTS:
-                own = block_ref.at[s, pl.ds(4 * q, 4), pl.ds(t * PS, PS), :]
+                own = block_ref.at[s, pl.ds(4 * q + LP * w, LP), pl.ds(t * PS, PS), :]
             if t == 0:
                 source = own
             else:
                 value = last[table[place[s] + e]]
                 if t < PARTS:
                     value = jnp.where(root[s], own[...], value)
-                source = stage.at[s, t - 1, e]
+                source = stage.at[s, w, t - 1, e]
                 source[...] = value
             pltpu.make_async_remote_copy(
-                src_ref=source, dst_ref=landing[s][t].at[e], send_sem=part_send, recv_sem=part_recv.at[s, t],
+                src_ref=source, dst_ref=landing[s][w][t].at[e], send_sem=part_send, recv_sem=part_recv.at[s, w, t],
                 device_id=peers[e], device_id_type=MESH).start()
 
     def assemble(s, c):
@@ -183,9 +185,9 @@
             late = table[place[s] + 8 + r]
             for p in range(4):
                 own = block_ref[s, 4 * r + p, pl.ds(c * PS, PS), :]
-                value = landing[s][c][way, p]
+                value = landing[s][p // LP][c][way, p % LP]
                 for d in range(1, DEPTH):
-                    value = jnp.where(late == d, landing[s][c + d][way, p], value)
+                    value = jnp.where(late == d, landing[s][p // LP][c + d][way, p % LP], value)
                 value = jnp.where(root[s], own, value)
                 got[4 * r + p] = value
                 got_turned[4 * r + p] = swapped(value) * pair_sign(PS)
@@ -222,11 +224,11 @@
         moved = [here]
         for i in range(1, 4):
             moved.append(pltpu.roll(jnp.where(lane < i, following, here), LANES - i, 1))
-        near = taps[s, 0, g, 0] * here[:n]
-        far = taps[s, 0, g, 4] * here
+        near = taps[s, 0, 0, g] * here[:n]
+        far = taps[s, 0, 4, g] * here
         for i in range(1, 4):
-            near = near + taps[s, 0, g, i] * moved[i][:n]
-            far = far + taps[s, 0, g, 4 + i] * moved[i]
+            near = near + taps[s, 0, i, g] * moved[i][:n]
+            far = far + taps[s, 0, 4 + i, g] * moved[i]
         shifted[g, pl.ds(0, wide), :] = far
         beyond = shifted[g, pl.ds(2, n), :]
         acc = near + pltpu.roll(jnp.where(lane[:n] < 4, beyond, far[:n]), LANES - 4, 1)
@@ -270,14 +272,14 @@
         def row0(g, _):
             first[g, span(k), :] = sub_ref[g, span(k), :] + added(0, g, k)
             return 0
-        lax.fori_loop(0, ROWS, row0, 0, unroll=4)
+        lax.fori_loop(0, ROWS, row0, 0, unroll=8)
         copy_core(k).start()
 
     def extend(k):
         def row1(g, _):
             second[g, span(k), :] = first[g, span(k), :] + added(1, g, k)
             return 0
-        lax.fori_loop(0, ROWS, row1, 0, unroll=4)
+        lax.fori_loop(0, ROWS, row1, 0, unroll=8)
 
     def meet(k):
         copy_core(k).wait_recv()
@@ -286,11 +288,10 @@
             second[g, span(k), :] = second[g, span(k), :] + rotated(first_in[g, span(k), :], 0, g)
             return 0
         lax.fori_loop(0, ROWS, row, 0, unroll=4)
+        copy_y(k).start()
 
     def finish(k):
         copy_y(k).wait_recv()
-        if k + WINDOW < CHUNKS:
-            copy_y(k + WINDOW).start()
         n = BOUNDS[k + 1] - BOUNDS[k]
 
         def row(g, _):
@@ -318,31 +319,49 @@
     pl.semaphore_wait(barrier, BEAMS + 1)
     for load in loads:
         load.wait()
+    def ready(s, k):
+        assemble(s, k)
+        project(s, k)
+
+    def section0(k):
+        if k < PARTS:
+            ready(0, k)
+        begin(k)
+
+    def section1(k):
+        if k < PARTS:
+            ready(1, k)
+        extend(k)
+
+    early = (STEPS - DEPTH) // 2
+    pieces = [functools.partial(prepare_rows, s, h * 8, h * 8 + 8) for s in range(2) for h in range(2)]
+    pieces += [prepare_slots] + [None] * (2 * DEPTH - 5)
+    for k in range(early + 1):
+        pieces += [functools.partial(ready, 0, k), functools.partial(begin, k)]
+        pieces += [functools.partial(ready, 1, k), functools.partial(extend, k)]
     for t in range(STEPS + 1):
         for s in range(2):
-            forward(s, t)
-        if t < 4:
-            prepare_rows(t // 2, t % 2 * 8, t % 2 * 8 + 8)
-        if t == 4:
-            prepare_slots()
-        c = t - DEPTH
-        if c >= 1:
-            meet(c - 1)
-            if c - 1 < WINDOW:
-                copy_y(c - 1).start()
-        if c >= 0:
-            assemble(0, c)
-            project(0, c)
-            begin(c)
-            assemble(1, c)
-            project(1, c)
-            extend(c)
-    begin(CHUNKS - 1)
-    extend(CHUNKS - 1)
-    meet(CHUNKS - 2)
-    meet(CHUNKS - 1)
-    for k in range(CHUNKS):
-        finish(k)
+            for w in range(LINES):
+                forward(s, w, t)
+            k, odd = divmod(t - DEPTH, 2)
+            if s == 0 and odd == 0 and 0 < k:
+                meet(k - 1)
+            if s == 0 and t == STEPS:
+                finish(0)
+            piece = pieces[2 * t + s]
+            if piece is not None:
+                piece()
+    for piece in pieces[2 * STEPS + 2 :]:
+        piece()
+    finish(1)
+    meet(early)
+    for k in range(early + 1, CHUNKS):
+        section0(k)
+        finish(k - 2)
+        section1(k)
+        meet(k)
+    finish(CHUNKS - 2)
+    finish(CHUNKS - 1)
 
     for s in range(2):
         own = block_ref.at[s, :, pl.ds(0, PS), :]
@@ -370,8 +389,8 @@
         out_shape=jax.ShapeDtypeStruct((SLOTS, SUBL, LANES), jnp.float32),
         in_specs=[smem] * 8 + [hbm] * 2,
         out_specs=hbm,
-        scratch_shapes=[vmem(4, 4, PS)] * (2 * STEPS) + [
-            vmem(2, STEPS - 1, 4, 4, PS),
+        scratch_shapes=[vmem(4, LP, PS)] * (2 * LINES * STEPS) + [
+            vmem(2, LINES, STEPS - 1, 4, LP, PS),
             vmem(ROWS, SUBL),
             vmem(2, PB, SUBL),
             vmem(PB, PS),
@@ -394,7 +413,7 @@
             pltpu.SMEM((SLOTS,), jnp.int32),
             pltpu.SemaphoreType.DMA((2,)),
             pltpu.SemaphoreType.DMA,
-            pltpu.SemaphoreType.DMA((2, STEPS)),
+            pltpu.SemaphoreType.DMA((2, LINES, STEPS)),
             pltpu.SemaphoreType.DMA((CHUNKS,)),
             pltpu.SemaphoreType.DMA((CHUNKS,)),
             pltpu.SemaphoreType.DMA((CHUNKS,)),
@@ -421,7 +440,7 @@
     subimage, pulses, ingest_owner, weights, offsets, filter_taps, cycles, merge_phase, destination
 ):
     out = call(
-        ingest_owner, weights, offsets, filter_taps, cycles, merge_phase, destination, jnp.asarray(tree_table()),
+        ingest_owner[:, 0], weights, offsets, filter_taps.transpose(0, 1, 3, 2), cycles, merge_phase, destination[:, 0], jnp.asarray(tree_table()),
         paired(subimage[0]), paired(pulses[:, 0, 0]),
     )
     out = out.reshape(SLOTS, SUBL // 2, 2, LANES).transpose(0, 2, 1, 3)

time: 126 us -> 104 us (0.83)
  Pallas kernels: 117 us -> 99.3 us
  local copies, waits for them, and re-layouts: 8.63 us -> 4.65 us
    pallas_call x1, Pallas kernels: 117 us -> 99.3 us  [call(): pl.pallas_call(kernel, out_shape=jax.ShapeDtypeStruct((SLOTS, SUBL, LANES...]
    unnamed x4 -> x1, local copies, waits for them, and re-layouts: 8.63 us -> 4.65 us
where the time goes in v4:
time: 104 us
  Pallas kernels  99.3 us (95%)
  local copies, waits for them, and re-layouts  4.65 us (4%)
    pallas_call x1, Pallas kernels, call(): pl.pallas_call(kernel, out_shape=jax.ShapeDtypeStruct((SLOTS, SUBL, LANES...  99.3 us
    unnamed x1, local copies, waits for them, and re-layouts  4.65 us

profile of v4, /device:TPU:0, one launch (start us, length us, event | category | flops | bytes accessed | tf_op | source)
XLA Modules:
  0.0 104.0 jit_solution(2182096845047430185)
XLA Ops:
  0.0 99.3 %shard_map.100 = f32[32,256,128]{2,1,0:T(8,128)} custom-call(s32[2]{0:T(128)} %bitcast.22, f32[2,1,16,2,16]{4,3,2,1,0:T(2,128)} %weights.1, s32[2,1,16]{2,1,0:T(1,128)} %offsets.1, f32[2,1,8,16]{3,2,1,0:T(8,128)} %bitcast.21, s32[2,1,16]{2,1,0:T(1,128)} %cycles.1, f32[2,1,16]{2,1,0:T(1,128)} %phases.1, s32[16]{0:T(128)} %bitcast.23, ...), custom_call_target="tpu_custom_call" | custom-call | tf_op jit(solution)/shard_map/pallas_call | solution.py:387
  99.3 4.7 %copy.15 = f32[1,32,2,16384]{3,2,1,0:T(2,128)} copy(f32[1,32,2,16384]{3,2,1,0:T(2,128)} %bitcast.18) | data formatting | bytes 8388608

commit v5 on v4

--- a/solution.py
+++ b/solution.py
@@ -36,6 +36,7 @@
 HALO = 16
 BOUNDS = [0] + [PS * i - HALO for i in range(1, PARTS + 1)] + [SUBL]
 CHUNKS = PARTS + 1
+SMALL = 8
 
 
 def tree_table():
@@ -84,12 +85,10 @@
     return cos, sin
 
 
-def kernel(
-    owner, weights, offsets, taps, cycles, phases, targets, table,
-    sub_hbm, pulse_hbm,
-    out_ref,
-    *scratch,
-):
+def kernel(*refs):
+    small, (sub_hbm, pulse_hbm, out_ref), scratch = refs[:SMALL], refs[SMALL : SMALL + 3], refs[SMALL + 3 :]
+    held, small_sem, scratch = scratch[:SMALL], scratch[SMALL], scratch[SMALL + 1 :]
+    owner, weights, offsets, taps, cycles, phases, targets, table = held
     landing = [[scratch[(s * LINES + w) * STEPS : (s * LINES + w + 1) * STEPS] for w in range(LINES)] for s in range(2)]
     (stage, sub_ref, block_ref, got, got_turned, proj, shifted, ramped, ramp_cos, ramp_sin, step_cos, step_sin,
      turn_cos, turn_sin, first, first_in, second, second_in, merged, slots, slot_row,
@@ -108,16 +107,13 @@
     for shift in range(1, BEAMS):
         pl.semaphore_signal(barrier, inc=1, device_id=(sub, me ^ shift), device_id_type=MESH)
 
+    fetches = [pltpu.make_async_copy(small[i], held[i], small_sem.at[i]) for i in range(SMALL)]
+    for fetch in fetches:
+        fetch.start()
     loads = [pltpu.make_async_copy(pulse_hbm, block_ref, load_sem.at[0]),
              pltpu.make_async_copy(sub_hbm, sub_ref, load_sem.at[1])]
     for load in loads:
         load.start()
-
-    place = []
-    for s in range(2):
-        o = owner[s]
-        place.append((((x - o // 4) & 3) * 4 + ((z - o % 4) & 3)) * 12)
-    root = [place[s] == 0 for s in range(2)]
 
     def prepare_rows(s, lo, hi):
         sublane = lax.broadcasted_iota(jnp.int32, (8, LANES), 0)
@@ -166,7 +162,8 @@
         for e in range(4):
             q = (e + 3) % 4
             if t < PARTS:
-                own = block_ref.at[s, pl.ds(4 * q + LP * w, LP), pl.ds(t * PS, PS), :]
+                held = pulse_hbm if t == 0 else block_ref
+                own = held.at[s, pl.ds(4 * q + LP * w, LP), pl.ds(t * PS, PS), :]
             if t == 0:
                 source = own
             else:
@@ -317,8 +314,6 @@
         copy_own(k).start()
 
     pl.semaphore_wait(barrier, BEAMS + 1)
-    for load in loads:
-        load.wait()
     def ready(s, k):
         assemble(s, k)
         project(s, k)
@@ -332,6 +327,14 @@
         if k < PARTS:
             ready(1, k)
         extend(k)
+
+    for fetch in fetches:
+        fetch.wait()
+    place = []
+    for s in range(2):
+        o = owner[s]
+        place.append((((x - o // 4) & 3) * 4 + ((z - o % 4) & 3)) * 12)
+    root = [place[s] == 0 for s in range(2)]
 
     early = (STEPS - DEPTH) // 2
     pieces = [functools.partial(prepare_rows, s, h * 8, h * 8 + 8) for s in range(2) for h in range(2)]
@@ -340,6 +343,9 @@
         pieces += [functools.partial(ready, 0, k), functools.partial(begin, k)]
         pieces += [functools.partial(ready, 1, k), functools.partial(extend, k)]
     for t in range(STEPS + 1):
+        if t == 1:
+            for load in loads:
+                load.wait()
         for s in range(2):
             for w in range(LINES):
                 forward(s, w, t)
@@ -378,7 +384,6 @@
 
 
 def call(*operands):
-    smem = pl.BlockSpec(memory_space=pltpu.SMEM)
     hbm = pl.BlockSpec(memory_space=pl.ANY)
 
     def vmem(*shape):
@@ -387,9 +392,11 @@
     return pl.pallas_call(
         kernel,
         out_shape=jax.ShapeDtypeStruct((SLOTS, SUBL, LANES), jnp.float32),
-        in_specs=[smem] * 8 + [hbm] * 2,
+        in_specs=[hbm] * (SMALL + 2),
         out_specs=hbm,
-        scratch_shapes=[vmem(4, LP, PS)] * (2 * LINES * STEPS) + [
+        scratch_shapes=[pltpu.SMEM(x.shape, x.dtype) for x in operands[:SMALL]] + [
+            pltpu.SemaphoreType.DMA((SMALL,)),
+        ] + [vmem(4, LP, PS)] * (2 * LINES * STEPS) + [
             vmem(2, LINES, STEPS - 1, 4, LP, PS),
             vmem(ROWS, SUBL),
             vmem(2, PB, SUBL),

time: 104 us -> 103 us (level)
  Pallas kernels: 99.3 us -> 97.9 us
    pallas_call x1, Pallas kernels: 99.3 us -> 97.9 us  [call(): pl.pallas_call(kernel, out_shape=jax.ShapeDtypeStruct((SLOTS, SUBL, LANES...]
where the time goes in v5:
time: 103 us
  Pallas kernels  97.9 us (95%)
  local copies, waits for them, and re-layouts  4.65 us (5%)
    pallas_call x1, Pallas kernels, call(): pl.pallas_call(kernel, out_shape=jax.ShapeDtypeStruct((SLOTS, SUBL, LANES...  97.9 us
    unnamed x1, local copies, waits for them, and re-layouts  4.65 us

profile of v5, /device:TPU:0, one launch (start us, length us, event | category | flops | bytes accessed | tf_op | source)
XLA Modules:
  0.0 102.5 jit_solution(7079120052119836380)
XLA Ops:
  0.0 97.9 %shard_map.100 = f32[32,256,128]{2,1,0:T(8,128)} custom-call(s32[2]{0:T(128)} %bitcast.22, f32[2,1,16,2,16]{4,3,2,1,0:T(2,128)} %refs_1_.1, s32[2,1,16]{2,1,0:T(1,128)} %refs_2_.1, f32[2,1,8,16]{3,2,1,0:T(8,128)} %bitcast.21, s32[2,1,16]{2,1,0:T(1,128)} %refs_4_.1, f32[2,1,16]{2,1,0:T(1,128)} %refs_5_.1, s32[16]{0:T(128)} %bitcast.23, ...), custom_call_target="tpu_custom_call" | custom-call | tf_op jit(solution)/shard_map/pallas_call | solution.py:392
  97.9 4.7 %copy.15 = f32[1,32,2,16384]{3,2,1,0:T(2,128)} copy(f32[1,32,2,16384]{3,2,1,0:T(2,128)} %bitcast.18) | data formatting | bytes 8388608
